TPU v7x, 256 devices: a whole 4x4x8 slice. The times are simulated.
256 devices in a mesh: row: 16 (over z, core), col: 16 (over y, x).
Axes of the slice: x: 4, y: 4, z: 8, core: 2. Of those that a mesh axis runs over, the one named last changes fastest.
Arguments:
- tokens: bfloat16 [1024, 12288], P('col', 'row'), may hold values from -6 to 6
- weight: bfloat16 [12288, 24576], P('row', 'col'), may hold values from -0.0546875 to 0.0546875
- cotangent: bfloat16 [1024, 24576], P('row', 'col'), may hold values from -6 to 6
Outputs:
- activated: bfloat16 [1024, 24576], P('row', 'col')
- input_grad: bfloat16 [1024, 12288], P('col', 'row')
- weight_grad: bfloat16 [12288, 24576], P('row', 'col')
All inputs are finite; a program needn't handle non-finite values.
Results may differ from a plain program's by a relative error of at most 0.03.
Values may be sent and summed in bfloat16 or wider, within the bound.
A program may use at most 64 MiB of HBM per device.

v0:
```python
import math

import jax
import jax.numpy as jnp
from jax import lax
from jax.sharding import PartitionSpec as P


def gelu_exact(value):
    return 0.5 * value * (1.0 + jax.scipy.special.erf(value / math.sqrt(2.0)))


def gelu_slope(value):
    return 0.5 * (1.0 + jax.scipy.special.erf(value / math.sqrt(2.0))) + value * jnp.exp(
        -0.5 * value * value
    ) / math.sqrt(2.0 * math.pi)


def on_device(tokens, weight, cotangent):
    gathered = lax.all_gather(tokens, "col", axis=0, tiled=True)
    block = gathered
    pre = lax.psum_scatter(
        jnp.dot(block, weight, preferred_element_type=jnp.float32).astype(jnp.bfloat16),
        "row",
        scatter_dimension=0,
        tiled=True,
    ).astype(jnp.float32)
    activated = gelu_exact(pre).astype(jnp.bfloat16)
    slope_grad = (cotangent.astype(jnp.float32) * gelu_slope(pre)).astype(jnp.bfloat16)
    grad_full = lax.all_gather(slope_grad, "row", axis=0, tiled=True)
    block = grad_full
    input_grad = lax.psum_scatter(
        lax.dot_general(
            block, weight, (((1,), (1,)), ((), ())), preferred_element_type=jnp.float32
        ).astype(jnp.bfloat16),
        "col",
        scatter_dimension=0,
        tiled=True,
    )
    weight_grad = lax.dot_general(
        gathered, grad_full, (((0,), (0,)), ((), ())), preferred_element_type=jnp.float32
    ).astype(jnp.bfloat16)
    return (activated, input_grad, weight_grad)


def solution(mesh):
    return jax.shard_map(
        on_device,
        mesh=mesh,
        in_specs=(P("col", "row"), P("row", "col"), P("row", "col")),
        out_specs=(P("row", "col"), P("col", "row"), P("row", "col")),
        check_vma=False,
    )
```

profile of v0, /device:TPU:6, one launch (start us, length us, event | category | flops | bytes accessed | tf_op | source)
XLA Modules:
  0.0 259.7 jit_solution(8037169074084997950)
XLA Ops:
  7.2 0.0 copy-start
  7.2 0.0 all-gather.3.cloned.1.call-start
  7.2 0.7 all-gather.3.cloned.1.call-update
  7.9 0.0 reduce-scatter.3.cloned.1.call-start
  8.0 54.0 %all-gather.3.cloned.1.call-done = bf16[1024,768]{1,0:T(8,128)(2,1)} async-done(((bf16[64,768]{1,0:T(8,128)(2,1)}), bf16[1024,768]{1,0:T(8,128)(2,1)}) %all-gather.3.cloned.1.call-update) | async-done | bytes 1572880 | tf_op jit(solution)/shard_map/all_gather | solution.py:20
  61.9 0.0 copy-done
  61.9 5.4 %convolution_convert_fusion = bf16[1024,1536]{1,0:T(8,128)(2,1)} fusion(bf16[1024,768]{1,0:T(8,128)(2,1)} %all-gather.3.cloned.1.call-done, bf16[768,1536]{1,0:T(8,128)(2,1)S(1)} %copy-done), kind=kOutput, calls=%fused_computation | convolution fusion | flops 2417491968 | bytes 7077888 | tf_op jit(solution)/shard_map/dot_general | solution.py:23
  67.4 0.0 copy-start.1
  67.4 0.0 reduce-scatter.3.cloned.1.call-update
  67.4 0.0 all-gather.5.cloned.1.call-start
  67.5 60.9 %reduce-scatter.3.cloned.1.call-done = bf16[64,1536]{1,0:T(8,128)(2,1)} async-done(((bf16[1024,1536]{1,0:T(8,128)(2,1)}), bf16[64,1536]{1,0:T(8,128)(2,1)}) %reduce-scatter.3.cloned.1.call-update) | async-done | bytes 196624 | tf_op jit(solution)/shard_map/reduce_scatter | solution.py:22
  128.4 0.0 copy-done.1
  128.4 1.9 fusion.9
  130.3 0.0 all-gather.5.cloned.1.call-update
  130.3 0.0 reduce-scatter.5.cloned.1.call-start
  130.4 40.0 %all-gather.5.cloned.1.call-done = bf16[1024,1536]{1,0:T(8,128)(2,1)} async-done(((bf16[64,1536]{1,0:T(8,128)(2,1)}), bf16[1024,1536]{1,0:T(8,128)(2,1)}) %all-gather.5.cloned.1.call-update) | async-done | bytes 3145744 | tf_op jit(solution)/shard_map/all_gather | solution.py:30
  170.3 5.7 %convolution_convert_fusion.2 = bf16[1024,768]{1,0:T(8,128)(2,1)} fusion(bf16[1024,1536]{1,0:T(8,128)(2,1)} %all-gather.5.cloned.1.call-done, bf16[768,1536]{1,0:T(8,128)(2,1)S(1)} %copy-done), kind=kOutput, calls=%fused_computation.3 | convolution fusion | flops 2416705536 | bytes 7077888 | tf_op jit(solution)/shard_map/dot_general | solution.py:33
  176.1 0.0 reduce-scatter.5.cloned.1.call-update
  176.1 6.5 %fusion = bf16[768,1536]{0,1:T(8,128)(2,1)} fusion(bf16[1024,1536]{1,0:T(8,128)(2,1)} %all-gather.5.cloned.1.call-done, bf16[1024,768]{1,0:T(8,128)(2,1)} %all-gather.3.cloned.1.call-done), kind=kOutput, calls=%fused_computation.2 | convolution fusion | flops 2417098752 | bytes 7077888 | tf_op jit(solution)/shard_map/dot_general | solution.py:40
  182.6 4.3 %copy.6 = bf16[768,1536]{1,0:T(8,128)(2,1)} copy(bf16[768,1536]{0,1:T(8,128)(2,1)} %fusion) | data formatting | bytes 4718592
  186.9 66.3 %reduce-scatter.5.cloned.1.call-done = bf16[64,768]{1,0:T(8,128)(2,1)} async-done(((bf16[1024,768]{1,0:T(8,128)(2,1)}), bf16[64,768]{1,0:T(8,128)(2,1)}) %reduce-scatter.5.cloned.1.call-update) | async-done | bytes 98320 | tf_op jit(solution)/shard_map/reduce_scatter | solution.py:32
Async XLA Ops:
  7.2 54.8 %copy-start = (bf16[768,1536]{1,0:T(8,128)(2,1)S(1)}, bf16[768,1536]{1,0:T(8,128)(2,1)}, u32[]{:S(2)}) copy-start(bf16[768,1536]{1,0:T(8,128)(2,1)} %param.4) | copy-start | bytes 7077892
  7.2 54.8 %all-gather.3.cloned.1.call-start = ((), (), s32[]{:S(2)}) async-start(), calls=%async_computation.2 | async-start | bytes 1671168 | tf_op jit(solution)/shard_map/all_gather | solution.py:20
  7.9 120.5 %reduce-scatter.3.cloned.1.call-start = ((), (), s32[]{:S(2)}) async-start(), calls=%async_computation.3 | async-start | bytes 3342336 | tf_op jit(solution)/shard_map/reduce_scatter | solution.py:22
  67.4 61.0 %copy-start.1 = (bf16[64,1536]{1,0:T(8,128)(2,1)S(1)}, bf16[64,1536]{1,0:T(8,128)(2,1)}, u32[]{:S(2)}) copy-start(bf16[64,1536]{1,0:T(8,128)(2,1)} %param.5) | copy-start | bytes 589828
  67.4 102.9 %all-gather.5.cloned.1.call-start = ((), (), s32[]{:S(2)}) async-start(), calls=%async_computation.4 | async-start | bytes 3342336 | tf_op jit(solution)/shard_map/all_gather | solution.py:30
  130.3 122.8 %reduce-scatter.5.cloned.1.call-start = ((), (), s32[]{:S(2)}) async-start(), calls=%async_computation.5 | async-start | bytes 1671168 | tf_op jit(solution)/shard_map/reduce_scatter | solution.py:32
Sparse Core Ops, SparseCore 0:
  10.4 51.4 all-gather.2
  67.5 60.8 reduce-scatter.2
  130.8 39.4 all-gather.4
  176.2 76.8 reduce-scatter.4
where the time goes:
time: 260 us
  waiting for transfers between devices  222 us (85%)
  matrix products  17.7 us (7%)
  between operations  13.8 us (5%)
  local copies, waits for them, and re-layouts  4.28 us (2%)
    reduce_scatter x1, waiting for transfers between devices, on_device(): lax.psum_scatter(lax.dot_general(block, weight, (((1,), (1,)), ((), ())),...  66.3 us
    reduce_scatter x1, waiting for transfers between devices, on_device(): lax.psum_scatter(jnp.dot(block, weight, preferred_element_type=jnp.float3...  60.9 us
    all_gather x1, waiting for transfers between devices, on_device(): gathered = lax.all_gather(tokens, 'col', axis=0, tiled=True)  54 us
    all_gather x1, waiting for transfers between devices, on_device(): grad_full = lax.all_gather(slope_grad, 'row', axis=0, tiled=True)  40 us
    dot_general x1, matrix products, on_device(): lax.dot_general(gathered, grad_full, (((0,), (0,)), ((), ())), preferred_...  6.51 us
    dot_general x1, matrix products, on_device(): lax.dot_general(block, weight, (((1,), (1,)), ((), ())), preferred_elemen...  5.75 us
    dot_general x1, matrix products, on_device(): jnp.dot(block, weight, preferred_element_type=jnp.float32)  5.44 us
  transfers between devices with their start and end apart: 4, of which 4 were waited for; matrix products, arithmetic and copies ran while one was open for 4% of the time, Pallas kernels for 0%

commit v1 on v0

v1 whole, which is shorter than its diff:
```python
import functools
import math

import jax
import jax.numpy as jnp
from jax import lax
from jax.experimental import pallas as pl
from jax.experimental.pallas import tpu as pltpu
from jax.sharding import PartitionSpec as P

MESH = pl.DeviceIdType.MESH
BF16 = jnp.bfloat16
F32 = jnp.float32

NR = 16
NC = 16
NZ = NR // 2
ROWS = 16
TILE = 256


def gelu_pair(value):
    phi = 0.5 * (1.0 + lax.erf(value * (1.0 / math.sqrt(2.0))))
    slope = phi + value * jnp.exp(-0.5 * value * value) * (1.0 / math.sqrt(2.0 * math.pi))
    return value * phi, slope


def kernel(
    stages,
    tok_ref, w_ref, cot_ref,
    act_ref, ig_ref, wg_ref,
    w, cot, tok, pp, px, s4, sp, sm, rp, rm, g, ip, r2, act, ig, wg,
    in_sem, out_sem,
    ag1_send, ag1_recv, px_send, px_recv,
    rs_send, rp_recv, rm_recv,
    ag_send, gp_recv, gm_recv, pt_send, pt_recv,
    r2_send, r2_recv,
):
    r, c = lax.axis_index("row"), lax.axis_index("col")
    z, k = r // 2, lax.rem(r, 2)
    other = 1 - k
    width, hidden = w.shape
    half = hidden // 2
    lo, hi = pl.ds(0, half), pl.ds(half, half)

    up = (lax.rem(r + 2, NR), c)
    down = (lax.rem(r + NR - 2, NR), c)
    partner = (r + 1 - 2 * k, c)

    def peer(i):
        return lax.rem(c + i, NC)

    def at_z(q):
        return lax.rem(z + q + NZ, NZ)

    def remote(src, dst, ss, rs, dev):
        cp = pltpu.make_async_remote_copy(
            src_ref=src, dst_ref=dst, send_sem=ss, recv_sem=rs,
            device_id=dev, device_id_type=MESH,
        )
        cp.start()

    def wait_for(ref, sem):
        pltpu.make_async_copy(ref, ref, sem).wait()

    loads = [
        pltpu.make_async_copy(w_ref, w, in_sem.at[0]),
        pltpu.make_async_copy(cot_ref, cot, in_sem.at[1]),
    ]
    for cp in loads:
        cp.start()

    barrier = pltpu.get_barrier_semaphore()
    greeted = [(r, peer(i)) for i in range(1, NC)] + [up, down, partner]
    for dev in greeted:
        pl.semaphore_signal(barrier, inc=1, device_id=dev, device_id_type=MESH)
    pl.semaphore_wait(barrier, len(greeted))

    for s in range(stages):
        block = tok_ref.at[pl.ds(s * ROWS, ROWS)]
        for i in range(1, NC):
            remote(block, tok.at[s, c], ag1_send.at[s], ag1_recv.at[s], (r, peer(i)))
        own = pltpu.make_async_copy(block, tok.at[s, c], in_sem.at[2 + s])
        own.start()
        loads.append(own)

    def m1(s):
        if s == 0:
            loads[0].wait()
        loads[2 + s].wait()
        wait_for(tok.at[s, pl.ds(0, NC - 1)], ag1_recv.at[s])

        def body(j, carry):
            cols = pl.ds(pl.multiple_of(j * TILE, TILE), TILE)
            left = tok[s].reshape(NC * ROWS, width)
            part = jnp.dot(left, w[:, cols], preferred_element_type=F32).astype(BF16)
            pp[s, :, :, :, cols] = part.reshape(NZ, 2, ROWS, TILE)
            return carry

        lax.fori_loop(0, hidden // TILE, body, 0)
        remote(pp.at[s, :, other], px.at[s], px_send.at[s], px_recv.at[s], partner)

    def base(s, d):
        return pp[s, d, k].astype(F32) + px[s, d].astype(F32)

    def r4(s):
        wait_for(px.at[s], px_recv.at[s])
        s4[s] = base(s, at_z(4)).astype(BF16)
        remote(s4.at[s, :, lo], rp.at[s, 3, :, lo], rs_send.at[s, 0], rp_recv.at[s, 3], up)
        remote(s4.at[s, :, hi], rm.at[s, 3, :, hi], rs_send.at[s, 1], rm_recv.at[s, 3], down)

    def r3(s):
        wait_for(rp.at[s, 3, :, lo], rp_recv.at[s, 3])
        up_sum = base(s, at_z(3))
        sp[s, 3, :, lo] = (up_sum[:, :half] + rp[s, 3, :, lo].astype(F32)).astype(BF16)
        sp[s, 3, :, hi] = up_sum[:, half:].astype(BF16)
        remote(sp.at[s, 3], rp.at[s, 2], rs_send.at[s, 2], rp_recv.at[s, 2], up)
        wait_for(rm.at[s, 3, :, hi], rm_recv.at[s, 3])
        down_sum = base(s, at_z(-3))
        sm[s, 3, :, hi] = (down_sum[:, half:] + rm[s, 3, :, hi].astype(F32)).astype(BF16)
        sm[s, 3, :, lo] = down_sum[:, :half].astype(BF16)
        remote(sm.at[s, 3], rm.at[s, 2], rs_send.at[s, 3], rm_recv.at[s, 2], down)

    def rj(s, j):
        wait_for(rp.at[s, j], rp_recv.at[s, j])
        sp[s, j] = (base(s, at_z(j)) + rp[s, j].astype(F32)).astype(BF16)
        remote(sp.at[s, j], rp.at[s, j - 1], rs_send.at[s, 8 - 2 * j], rp_recv.at[s, j - 1], up)
        wait_for(rm.at[s, j], rm_recv.at[s, j])
        sm[s, j] = (base(s, at_z(-j)) + rm[s, j].astype(F32)).astype(BF16)
        remote(sm.at[s, j], rm.at[s, j - 1], rs_send.at[s, 9 - 2 * j], rm_recv.at[s, j - 1], down)

    def r0(s):
        wait_for(rp.at[s, 0], rp_recv.at[s, 0])
        wait_for(rm.at[s, 0], rm_recv.at[s, 0])
        if s == 0:
            loads[1].wait()
        rows = pl.ds(s * ROWS, ROWS)
        pre = base(s, z) + rp[s, 0].astype(F32) + rm[s, 0].astype(F32)
        activated, slope = gelu_pair(pre)
        g[s, z, k] = (cot[rows].astype(F32) * slope).astype(BF16)
        mine = g.at[s, z, k]
        remote(mine, mine, ag_send.at[s, 0], gp_recv.at[s, 0], up)
        remote(mine, mine, ag_send.at[s, 1], gm_recv.at[s, 0], down)
        remote(mine, mine, pt_send.at[s], pt_recv.at[s], partner)
        act[rows] = activated.astype(BF16)

    def a(s, j):
        below, above = g.at[s, at_z(-j), k], g.at[s, at_z(j), k]
        if j < 3:
            wait_for(below, gp_recv.at[s, j - 1])
            remote(below, below, ag_send.at[s, 2 * j], gp_recv.at[s, j], up)
            wait_for(above, gm_recv.at[s, j - 1])
            remote(above, above, ag_send.at[s, 2 * j + 1], gm_recv.at[s, j], down)
        else:
            wait_for(below, gp_recv.at[s, j - 1])
            part = g.at[s, at_z(-j), k, :, lo]
            remote(part, part, ag_send.at[s, 2 * j], gp_recv.at[s, j], up)
            wait_for(above, gm_recv.at[s, j - 1])
            part = g.at[s, at_z(j), k, :, hi]
            remote(part, part, ag_send.at[s, 2 * j + 1], gm_recv.at[s, j], down)
        remote(below, below, pt_send.at[s], pt_recv.at[s], partner)
        remote(above, above, pt_send.at[s], pt_recv.at[s], partner)

    def a4(s):
        far = g.at[s, at_z(4), k]
        wait_for(g.at[s, at_z(4), k, :, lo], gp_recv.at[s, 3])
        wait_for(g.at[s, at_z(4), k, :, hi], gm_recv.at[s, 3])
        remote(far, far, pt_send.at[s], pt_recv.at[s], partner)

    def m2(s):
        wait_for(g.at[s, :, other], pt_recv.at[s])

        def body(j, carry):
            cols = pl.ds(pl.multiple_of(j * TILE, TILE), TILE)
            left = g[s].reshape(NR * ROWS, hidden)
            part = lax.dot_general(
                left, w[cols, :], (((1,), (1,)), ((), ())), preferred_element_type=F32
            ).astype(BF16)
            ip[s, :, :, cols] = part.reshape(NC, ROWS, TILE)
            return carry

        lax.fori_loop(0, width // TILE, body, 0)
        for i in range(1, NC):
            remote(ip.at[s, peer(i)], r2.at[s, i - 1], r2_send.at[s], r2_recv.at[s], (r, peer(i)))

    def fin(s):
        wait_for(r2.at[s], r2_recv.at[s])
        total = ip[s, c].astype(F32)
        for i in range(NC - 1):
            total += r2[s, i].astype(F32)
        ig[pl.ds(s * ROWS, ROWS)] = total.astype(BF16)

    def wgrad():
        def body(j, carry):
            cols = pl.ds(pl.multiple_of(j * TILE, TILE), TILE)
            left = tok[...].reshape(stages * NC * ROWS, width)
            right = g[:, :, :, :, cols].reshape(stages * NR * ROWS, TILE)
            wg[:, cols] = lax.dot_general(
                left, right, (((0,), (0,)), ((), ())), preferred_element_type=F32
            ).astype(BF16)
            return carry

        lax.fori_loop(0, hidden // TILE, body, 0)

    steps = [
        m1, r4, r3,
        lambda s: rj(s, 2), lambda s: rj(s, 1), r0,
        lambda s: a(s, 1), lambda s: a(s, 2), lambda s: a(s, 3), a4, m2,
    ]
    for t in range(len(steps) + stages - 1):
        for s in range(stages):
            if 0 <= t - s < len(steps):
                steps[t - s](s)
    outs = [pltpu.make_async_copy(act, act_ref, out_sem.at[0])]
    outs[0].start()
    wgrad()
    outs.append(pltpu.make_async_copy(wg, wg_ref, out_sem.at[1]))
    outs[1].start()
    for s in range(stages):
        fin(s)
    outs.append(pltpu.make_async_copy(ig, ig_ref, out_sem.at[2]))
    outs[2].start()

    for s in range(stages):
        wait_for(tok.at[s, pl.ds(0, NC - 1)], ag1_send.at[s])
        wait_for(px.at[s], px_send.at[s])
        wait_for(s4.at[s, :, lo], rs_send.at[s, 0])
        wait_for(s4.at[s, :, hi], rs_send.at[s, 1])
        for j in range(2, 8):
            wait_for(s4.at[s], rs_send.at[s, j])
        for j in range(6):
            wait_for(s4.at[s], ag_send.at[s, j])
        wait_for(s4.at[s, :, lo], ag_send.at[s, 6])
        wait_for(s4.at[s, :, hi], ag_send.at[s, 7])
        wait_for(g.at[s, :, 0], pt_send.at[s])
        wait_for(r2.at[s], r2_send.at[s])
    for cp in outs:
        cp.wait()


def on_device(tokens, weight, cotangent):
    rows, width = tokens.shape
    hidden = weight.shape[1]
    stages = rows // ROWS
    vmem, dma = pltpu.VMEM, pltpu.SemaphoreType.DMA
    any_spec = pl.BlockSpec(memory_space=pl.ANY)
    return tuple(pl.pallas_call(
        functools.partial(kernel, stages),
        out_shape=(
            jax.ShapeDtypeStruct((rows, hidden), BF16),
            jax.ShapeDtypeStruct((rows, width), BF16),
            jax.ShapeDtypeStruct((width, hidden), BF16),
        ),
        in_specs=[any_spec] * 3,
        out_specs=(any_spec,) * 3,
        scratch_shapes=[
            vmem((width, hidden), BF16),
            vmem((rows, hidden), BF16),
            vmem((stages, NC, ROWS, width), BF16),
            vmem((stages, NZ, 2, ROWS, hidden), BF16),
            vmem((stages, NZ, ROWS, hidden), BF16),
            vmem((stages, ROWS, hidden), BF16),
            vmem((stages, 4, ROWS, hidden), BF16),
            vmem((stages, 4, ROWS, hidden), BF16),
            vmem((stages, 4, ROWS, hidden), BF16),
            vmem((stages, 4, ROWS, hidden), BF16),
            vmem((stages, NZ, 2, ROWS, hidden), BF16),
            vmem((stages, NC, ROWS, width), BF16),
            vmem((stages, NC - 1, ROWS, width), BF16),
            vmem((rows, hidden), BF16),
            vmem((rows, width), BF16),
            vmem((width, hidden), BF16),
            dma((2 + stages,)), dma((3,)),
            dma((stages,)), dma((stages,)), dma((stages,)), dma((stages,)),
            dma((stages, 8)), dma((stages, 4)), dma((stages, 4)),
            dma((stages, 8)), dma((stages, 4)), dma((stages, 4)),
            dma((stages,)), dma((stages,)),
            dma((stages,)), dma((stages,)),
        ],
        compiler_params=pltpu.CompilerParams(
            collective_id=0, has_side_effects=True, vmem_limit_bytes=56 * 2**20
        ),
        name="updown",
    )(tokens, weight, cotangent))


def solution(mesh):
    return jax.shard_map(
        on_device,
        mesh=mesh,
        in_specs=(P("col", "row"), P("row", "col"), P("row", "col")),
        out_specs=(P("row", "col"), P("col", "row"), P("row", "col")),
        check_vma=False,
    )
```

time: 260 us -> 86.8 us (0.33)
  waiting for transfers between devices: 222 us -> 0 us
  Pallas kernels: 0 us -> 78.3 us
  matrix products: 17.7 us -> 0 us
  between operations: 13.8 us -> 0.64 us
    reduce_scatter x2 -> x0, waiting for transfers between devices: 127 us -> none  [the longest x1 66.3 us: on_device(): lax.psum_scatter(lax.dot_general(block, weight, (((1,), (1,)), ((), ())),...]
    all_gather x2 -> x0, waiting for transfers between devices: 93.9 us -> none  [the longest x1 54 us: on_device(): gathered = lax.all_gather(tokens, 'col', axis=0, tiled=True)]
    pallas_call x0 -> x1, Pallas kernels: none -> 78.3 us  [on_device(): pl.pallas_call(functools.partial(kernel, stages), out_shape=(jax.ShapeDty...]
    dot_general x3 -> x0, matrix products: 17.7 us -> none  [the longest x1 6.51 us: on_device(): lax.dot_general(gathered, grad_full, (((0,), (0,)), ((), ())), preferred_...]
    unnamed x5 -> x3, local copies, waits for them, and re-layouts: 4.28 us -> 6.38 us
  transfers between devices with their start and end apart: 4 -> 0, of which waited for: 4 -> 0; matrix products, arithmetic and copies ran while one was open for 4% -> 0% of each run, Pallas kernels for 0% -> 0%
where the time goes in v1:
time: 86.8 us; the launch traced here: 85.4 us
  Pallas kernels  78.3 us (90%)
  local copies, waits for them, and re-layouts  6.38 us (7%)
    pallas_call x1, Pallas kernels, on_device(): pl.pallas_call(functools.partial(kernel, stages), out_shape=(jax.ShapeDty...  78.3 us
    unnamed x3, local copies, waits for them, and re-layouts  6.38 us

profile of v1, /device:TPU:6, one launch (start us, length us, event | category | flops | bytes accessed | tf_op | source)
XLA Modules:
  0.0 85.4 jit_solution(15829438930613911052)
XLA Ops:
  0.6 78.3 %updown.1 = (bf16[64,1536]{1,0:T(8,128)(2,1)}, bf16[64,768]{1,0:T(8,128)(2,1)}, bf16[768,1536]{1,0:T(8,128)(2,1)}) custom-call(bf16[64,768]{1,0:T(8,128)(2,1)} %tok_ref.1, bf16[768,1536]{1,0:T(8,128)(2,1)} %w_ref.1, bf16[64,1536]{1,0:T(8,128)(2,1)} %cot_ref.1), custom_call_target="tpu_custom_call" | custom-call | tf_op jit(solution)/shard_map/updown/pallas_call | solution.py:247
  79.0 1.6 %copy.9 = bf16[64,1536]{1,0:T(8,128)(2,1)} copy(bf16[64,1536]{1,0:T(8,128)(2,1)} %get-tuple-element.6) | data formatting | bytes 393216
  80.6 1.5 %copy.10 = bf16[64,768]{1,0:T(8,128)(2,1)} copy(bf16[64,768]{1,0:T(8,128)(2,1)} %get-tuple-element.7) | data formatting | bytes 196608
  82.1 3.2 %copy.11 = bf16[768,1536]{1,0:T(8,128)(2,1)} copy(bf16[768,1536]{1,0:T(8,128)(2,1)} %get-tuple-element.8) | data formatting | bytes 4718592

commit v2 on v1

--- a/solution.py
+++ b/solution.py
@@ -16,7 +16,21 @@
 NC = 16
 NZ = NR // 2
 ROWS = 16
-TILE = 256
+TILE = 512
+
+CUTS = {1: ((0, 1, 2, 3, 4),), 2: ((0, 1, 2), (3, 4)), 3: ((0, 1, 2), (3,), (4,)), 4: ((0, 1), (2,), (3,), (4,))}
+PIECES = (1, 1, 1, 1)
+TWO = (1, 1, 1, 1)
+DIRECT = (0, 0, 0, 0)
+ORDER = (
+    ("O", 0), ("O", 1), ("O", 2), ("O", 3), ("F", 0), ("F", 1), ("F", 2), ("F", 3), ("M", 0), ("M", 1),
+    ("R4", 0), ("M", 2), ("R4", 1), ("M", 3), ("R3", 0), ("R4", 2), ("R3", 1), ("R4", 3), ("R2", 0), ("R3", 2),
+    ("R2", 1), ("R3", 3), ("R1", 0), ("R2", 2), ("R1", 1), ("R2", 3), ("R0", 0), ("R1", 2), ("R0", 1),
+    ("R1", 3), ("A1", 0), ("R0", 2), ("A1", 1), ("R0", 3), ("A2", 0), ("A1", 2), ("A2", 1), ("A1", 3),
+    ("A3", 0), ("A2", 2), ("A3", 1), ("A2", 3), ("A4", 0), ("A3", 2), ("A4", 1), ("A3", 3), ("N0", 0),
+    ("A4", 2), ("N0", 1), ("A4", 3), ("N0", 2), ("WG", 0), ("P", 0), ("N0", 3), ("P", 1), ("P", 2), ("P", 3),
+    ("WG", 1), ("FIN", 0), ("FIN", 1), ("FIN", 2), ("FIN", 3),
+)
 
 
 def gelu_pair(value):
@@ -29,12 +43,12 @@
     stages,
     tok_ref, w_ref, cot_ref,
     act_ref, ig_ref, wg_ref,
-    w, cot, tok, pp, px, s4, sp, sm, rp, rm, g, ip, r2, act, ig, wg,
+    w, cot, tok, pp, px, s4, sp, sm, rp, rm, g, ip, r2, t0, t1, act, ig, wg, acc,
     in_sem, out_sem,
-    ag1_send, ag1_recv, px_send, px_recv,
+    ag1_send, ag1a_recv, ag1b_recv, px_send, px_recv,
     rs_send, rp_recv, rm_recv,
     ag_send, gp_recv, gm_recv, pt_send, pt_recv,
-    r2_send, r2_recv,
+    r2_send, r2_recv, r2b_send, r2b_recv,
 ):
     r, c = lax.axis_index("row"), lax.axis_index("col")
     z, k = r // 2, lax.rem(r, 2)
@@ -50,6 +64,10 @@
     def peer(i):
         return lax.rem(c + i, NC)
 
+    def shift(da, db):
+        dx, dy = da + k * (db - da), db + k * (da - db)
+        return lax.rem(c // 4 + dy + 4, 4) * 4 + lax.rem(c + dx + 4, 4)
+
     def at_z(q):
         return lax.rem(z + q + NZ, NZ)
 
@@ -71,33 +89,46 @@
         cp.start()
 
     barrier = pltpu.get_barrier_semaphore()
-    greeted = [(r, peer(i)) for i in range(1, NC)] + [up, down, partner]
+    if any(DIRECT) or not all(TWO):
+        greeted = [(r, peer(i)) for i in range(1, NC)]
+    else:
+        greeted = [(r, shift(i, 0)) for i in (1, 2, 3)] + [(r, shift(0, i)) for i in (1, 2, 3)]
+    greeted += [up, down, partner]
     for dev in greeted:
         pl.semaphore_signal(barrier, inc=1, device_id=dev, device_id_type=MESH)
     pl.semaphore_wait(barrier, len(greeted))
 
-    for s in range(stages):
+    own_copies = {}
+
+    def own(s):
         block = tok_ref.at[pl.ds(s * ROWS, ROWS)]
-        for i in range(1, NC):
-            remote(block, tok.at[s, c], ag1_send.at[s], ag1_recv.at[s], (r, peer(i)))
-        own = pltpu.make_async_copy(block, tok.at[s, c], in_sem.at[2 + s])
-        own.start()
-        loads.append(own)
+        if DIRECT[s]:
+            for i in range(1, NC):
+                remote(block, tok.at[s, c], ag1_send.at[s], ag1b_recv.at[s], (r, peer(i)))
+        else:
+            for i in (1, 3, 2):
+                remote(block, tok.at[s, c], ag1_send.at[s], ag1a_recv.at[s, i - 1], (r, shift(i, 0)))
+            for i in (1, 3, 2):
+                remote(block, tok.at[s, c], ag1_send.at[s], ag1b_recv.at[s], (r, shift(0, i)))
+        cp = pltpu.make_async_copy(block, tok.at[s, c], in_sem.at[2 + s])
+        cp.start()
+        own_copies[s] = cp
+
+    def forward(s):
+        for i in (1, 3, 2):
+            block = tok.at[s, shift(-i, 0)]
+            wait_for(block, ag1a_recv.at[s, i - 1])
+            for j in (1, 3, 2):
+                remote(block, block, ag1_send.at[s], ag1b_recv.at[s], (r, shift(0, j)))
 
     def m1(s):
         if s == 0:
             loads[0].wait()
-        loads[2 + s].wait()
-        wait_for(tok.at[s, pl.ds(0, NC - 1)], ag1_recv.at[s])
-
-        def body(j, carry):
-            cols = pl.ds(pl.multiple_of(j * TILE, TILE), TILE)
-            left = tok[s].reshape(NC * ROWS, width)
-            part = jnp.dot(left, w[:, cols], preferred_element_type=F32).astype(BF16)
-            pp[s, :, :, :, cols] = part.reshape(NZ, 2, ROWS, TILE)
-            return carry
-
-        lax.fori_loop(0, hidden // TILE, body, 0)
+        own_copies[s].wait()
+        wait_for(tok.at[s, pl.ds(0, 15 if DIRECT[s] else 12)], ag1b_recv.at[s])
+        left = tok[s].reshape(NC * ROWS, width)
+        part = jnp.dot(left, w[...], preferred_element_type=F32).astype(BF16)
+        pp[s] = part.reshape(NZ, 2, ROWS, hidden)
         remote(pp.at[s, :, other], px.at[s], px_send.at[s], px_recv.at[s], partner)
 
     def base(s, d):
@@ -141,7 +172,7 @@
         mine = g.at[s, z, k]
         remote(mine, mine, ag_send.at[s, 0], gp_recv.at[s, 0], up)
         remote(mine, mine, ag_send.at[s, 1], gm_recv.at[s, 0], down)
-        remote(mine, mine, pt_send.at[s], pt_recv.at[s], partner)
+        remote(mine, mine, pt_send.at[s], pt_recv.at[s, 0], partner)
         act[rows] = activated.astype(BF16)
 
     def a(s, j):
@@ -158,67 +189,121 @@
             wait_for(above, gm_recv.at[s, j - 1])
             part = g.at[s, at_z(j), k, :, hi]
             remote(part, part, ag_send.at[s, 2 * j + 1], gm_recv.at[s, j], down)
-        remote(below, below, pt_send.at[s], pt_recv.at[s], partner)
-        remote(above, above, pt_send.at[s], pt_recv.at[s], partner)
+        remote(below, below, pt_send.at[s], pt_recv.at[s, 2 * j - 1], partner)
+        remote(above, above, pt_send.at[s], pt_recv.at[s, 2 * j], partner)
 
     def a4(s):
         far = g.at[s, at_z(4), k]
         wait_for(g.at[s, at_z(4), k, :, lo], gp_recv.at[s, 3])
         wait_for(g.at[s, at_z(4), k, :, hi], gm_recv.at[s, 3])
-        remote(far, far, pt_send.at[s], pt_recv.at[s], partner)
-
-    def m2(s):
-        wait_for(g.at[s, :, other], pt_recv.at[s])
-
-        def body(j, carry):
-            cols = pl.ds(pl.multiple_of(j * TILE, TILE), TILE)
-            left = g[s].reshape(NR * ROWS, hidden)
-            part = lax.dot_general(
-                left, w[cols, :], (((1,), (1,)), ((), ())), preferred_element_type=F32
-            ).astype(BF16)
-            ip[s, :, :, cols] = part.reshape(NC, ROWS, TILE)
-            return carry
-
-        lax.fori_loop(0, width // TILE, body, 0)
-        for i in range(1, NC):
-            remote(ip.at[s, peer(i)], r2.at[s, i - 1], r2_send.at[s], r2_recv.at[s], (r, peer(i)))
+        remote(far, far, pt_send.at[s], pt_recv.at[s, 7], partner)
+
+    def spread(s):
+        left = g[s].reshape(NR * ROWS, hidden)
+        part = lax.dot_general(
+            left, w[...], (((1,), (1,)), ((), ())), preferred_element_type=F32
+        ).astype(BF16)
+        ip[s] = part.reshape(NC, ROWS, width)
+        for i in (1, 3, 2):
+            for j in range(4):
+                remote(
+                    ip.at[s, shift(i, j)], r2.at[s, 4 * i - 4 + j],
+                    r2_send.at[s], r2_recv.at[s], (r, shift(i, 0)),
+                )
+
+    def pass_on(s):
+        wait_for(r2.at[s, pl.ds(0, 12)], r2_recv.at[s])
+        for j in (1, 3, 2, 0):
+            total = ip[s, shift(0, j)].astype(F32)
+            for i in range(3):
+                total += r2[s, 4 * i + j].astype(F32)
+            if j == 0:
+                t0[s] = total
+            else:
+                t1[s, j - 1] = total.astype(BF16)
+                remote(t1.at[s, j - 1], r2.at[s, 11 + j], r2b_send.at[s], r2b_recv.at[s], (r, shift(0, j)))
+
+    def m2_part(s, chunks):
+        for q, slot in chunks:
+            wait_for(g.at[s, 0, 0], pt_recv.at[s, slot])
+        if TWO[s]:
+            return spread(s)
+        left = jnp.concatenate(
+            [g[s, at_z(q)].reshape(2 * ROWS, hidden) for q, _ in chunks], axis=0
+        )
+        part = lax.dot_general(
+            left, w[...], (((1,), (1,)), ((), ())), preferred_element_type=F32
+        ).astype(BF16)
+        part = part.reshape(len(chunks), 2, ROWS, width)
+        for n, (q, _) in enumerate(chunks):
+            d = at_z(q)
+            ip[s, pl.ds(2 * d, 2)] = part[n]
+            for m in range(2):
+                dest = 2 * d + m
+
+                @pl.when(dest != c)
+                def _():
+                    slot = lax.rem(dest - c + NC, NC) - 1
+                    remote(ip.at[s, dest], r2.at[s, slot], r2_send.at[s], r2_recv.at[s], (r, dest))
 
     def fin(s):
+        if TWO[s]:
+            wait_for(r2.at[s, pl.ds(12, 3)], r2b_recv.at[s])
+            total = t0[s]
+            for j in range(3):
+                total += r2[s, 12 + j].astype(F32)
+            ig[pl.ds(s * ROWS, ROWS)] = total.astype(BF16)
+            return
         wait_for(r2.at[s], r2_recv.at[s])
         total = ip[s, c].astype(F32)
         for i in range(NC - 1):
             total += r2[s, i].astype(F32)
         ig[pl.ds(s * ROWS, ROWS)] = total.astype(BF16)
 
-    def wgrad():
+    def wgrad(part):
+        some = pl.ds(2 * part, 2)
+
         def body(j, carry):
             cols = pl.ds(pl.multiple_of(j * TILE, TILE), TILE)
-            left = tok[...].reshape(stages * NC * ROWS, width)
-            right = g[:, :, :, :, cols].reshape(stages * NR * ROWS, TILE)
-            wg[:, cols] = lax.dot_general(
+            left = tok[some].reshape(2 * NC * ROWS, width)
+            right = g[some, :, :, :, cols].reshape(2 * NR * ROWS, TILE)
+            total = lax.dot_general(
                 left, right, (((0,), (0,)), ((), ())), preferred_element_type=F32
-            ).astype(BF16)
+            )
+            if part == 0:
+                acc[:, cols] = total
+            else:
+                wg[:, cols] = (acc[:, cols] + total).astype(BF16)
             return carry
 
         lax.fori_loop(0, hidden // TILE, body, 0)
 
-    steps = [
-        m1, r4, r3,
-        lambda s: rj(s, 2), lambda s: rj(s, 1), r0,
-        lambda s: a(s, 1), lambda s: a(s, 2), lambda s: a(s, 3), a4, m2,
+    def product(s, n):
+        chunks = []
+        for j in CUTS[PIECES[s]][n]:
+            chunks += [(0, 0)] if j == 0 else [(4, 7)] if j == 4 else [(-j, 2 * j - 1), (j, 2 * j)]
+        m2_part(s, chunks)
+
+    outs = [
+        pltpu.make_async_copy(a_v, b_v, out_sem.at[n])
+        for n, (a_v, b_v) in enumerate(((act, act_ref), (wg, wg_ref), (ig, ig_ref)))
     ]
-    for t in range(len(steps) + stages - 1):
-        for s in range(stages):
-            if 0 <= t - s < len(steps):
-                steps[t - s](s)
-    outs = [pltpu.make_async_copy(act, act_ref, out_sem.at[0])]
-    outs[0].start()
-    wgrad()
-    outs.append(pltpu.make_async_copy(wg, wg_ref, out_sem.at[1]))
-    outs[1].start()
-    for s in range(stages):
-        fin(s)
-    outs.append(pltpu.make_async_copy(ig, ig_ref, out_sem.at[2]))
+
+    def start_wgrad(part):
+        wgrad(part)
+        if part == 1:
+            outs[0].start()
+            outs[1].start()
+
+    step = {"O": own, "F": forward, "M": m1, "R4": r4, "R3": r3, "R0": r0, "A4": a4, "P": pass_on, "FIN": fin, "WG": start_wgrad}
+    for j in (1, 2):
+        step[f"R{j}"] = functools.partial(lambda j, s: rj(s, j), j)
+    for j in (1, 2, 3):
+        step[f"A{j}"] = functools.partial(lambda j, s: a(s, j), j)
+    for n in range(4):
+        step[f"N{n}"] = functools.partial(lambda n, s: product(s, n), n)
+    for name, s in ORDER:
+        step[name](s)
     outs[2].start()
 
     for s in range(stages):
@@ -233,18 +318,30 @@
         wait_for(s4.at[s, :, lo], ag_send.at[s, 6])
         wait_for(s4.at[s, :, hi], ag_send.at[s, 7])
         wait_for(g.at[s, :, 0], pt_send.at[s])
-        wait_for(r2.at[s], r2_send.at[s])
+        if TWO[s]:
+            wait_for(r2.at[s, pl.ds(0, 12)], r2_send.at[s])
+            wait_for(r2.at[s, pl.ds(12, 3)], r2b_send.at[s])
+        else:
+            wait_for(r2.at[s], r2_send.at[s])
     for cp in outs:
         cp.wait()
 
 
-def on_device(tokens, weight, cotangent):
+def copy_kernel(*refs):
+    copies = [pltpu.make_async_copy(refs[n], refs[3 + n], refs[6].at[n]) for n in range(3)]
+    for cp in copies:
+        cp.start()
+    for cp in copies:
+        cp.wait()
+
+
+def kern(tokens, weight, cotangent):
     rows, width = tokens.shape
     hidden = weight.shape[1]
     stages = rows // ROWS
     vmem, dma = pltpu.VMEM, pltpu.SemaphoreType.DMA
     any_spec = pl.BlockSpec(memory_space=pl.ANY)
-    return tuple(pl.pallas_call(
+    return pl.pallas_call(
         functools.partial(kernel, stages),
         out_shape=(
             jax.ShapeDtypeStruct((rows, hidden), BF16),
@@ -267,21 +364,38 @@
             vmem((stages, NZ, 2, ROWS, hidden), BF16),
             vmem((stages, NC, ROWS, width), BF16),
             vmem((stages, NC - 1, ROWS, width), BF16),
+            vmem((stages, ROWS, width), F32),
+            vmem((stages, 3, ROWS, width), BF16),
             vmem((rows, hidden), BF16),
             vmem((rows, width), BF16),
             vmem((width, hidden), BF16),
+            vmem((width, hidden), F32),
             dma((2 + stages,)), dma((3,)),
-            dma((stages,)), dma((stages,)), dma((stages,)), dma((stages,)),
+            dma((stages,)), dma((stages, 3)), dma((stages,)), dma((stages,)), dma((stages,)),
             dma((stages, 8)), dma((stages, 4)), dma((stages, 4)),
             dma((stages, 8)), dma((stages, 4)), dma((stages, 4)),
-            dma((stages,)), dma((stages,)),
-            dma((stages,)), dma((stages,)),
+            dma((stages,)), dma((stages, 8)),
+            dma((stages,)), dma((stages,)), dma((stages,)), dma((stages,)),
         ],
         compiler_params=pltpu.CompilerParams(
-            collective_id=0, has_side_effects=True, vmem_limit_bytes=56 * 2**20
+            collective_id=0, has_side_effects=True, vmem_limit_bytes=50 * 2**20
         ),
         name="updown",
-    )(tokens, weight, cotangent))
+    )(tokens, weight, cotangent)
+
+
+def on_device(tokens, weight, cotangent):
+    outs = kern(tokens, weight, cotangent)
+    any_spec, dma = pl.BlockSpec(memory_space=pl.ANY), pltpu.SemaphoreType.DMA
+    return tuple(pl.pallas_call(
+        copy_kernel,
+        out_shape=tuple(jax.ShapeDtypeStruct(o.shape, o.dtype) for o in outs),
+        in_specs=[any_spec] * 3,
+        out_specs=(any_spec,) * 3,
+        scratch_shapes=[dma((3,))],
+        compiler_params=pltpu.CompilerParams(vmem_limit_bytes=16 * 2**20),
+        name="leave",
+    )(*outs))
 
 
 def solution(mesh):

time: 86.8 us -> 78.4 us (0.903); the launches traced: 85.4 us -> 78 us
  local copies, waits for them, and re-layouts: 6.38 us -> 1.81 us
  Pallas kernels: 78.3 us -> 75.5 us
    unnamed x3 -> x4, local copies, waits for them, and re-layouts: 6.38 us -> 1.81 us
    pallas_call x1 -> x2, Pallas kernels: 78.3 us -> 75.5 us  [the longest x1 74 us: kern(): pl.pallas_call(functools.partial(kernel, stages), out_shape=(jax.ShapeDty...]
where the time goes in v2:
time: 78.4 us; the launch traced here: 78 us
  Pallas kernels  75.5 us (96%)
  local copies, waits for them, and re-layouts  1.81 us (2%)
    pallas_call x1, Pallas kernels, kern(): pl.pallas_call(functools.partial(kernel, stages), out_shape=(jax.ShapeDty...  74 us
    unnamed x4, local copies, waits for them, and re-layouts  1.81 us

profile of v2, /device:TPU:6, one launch (start us, length us, event | category | flops | bytes accessed | tf_op | source)
XLA Modules:
  0.0 78.0 jit_solution(10920096088637451547)
XLA Ops:
  0.6 0.0 copy-start
  0.6 0.9 %copy-done = bf16[64,1536]{1,0:T(8,128)(2,1)S(1)} copy-done((bf16[64,1536]{1,0:T(8,128)(2,1)S(1)}, bf16[64,1536]{1,0:T(8,128)(2,1)}, u32[]{:S(2)}) %copy-start) | copy-done | bytes 196632
  1.6 0.0 copy-start.1
  1.6 0.9 %copy-done.1 = bf16[64,768]{1,0:T(8,128)(2,1)S(1)} copy-done((bf16[64,768]{1,0:T(8,128)(2,1)S(1)}, bf16[64,768]{1,0:T(8,128)(2,1)}, u32[]{:S(2)}) %copy-start.1) | copy-done | bytes 98328
  2.5 74.0 %updown.1 = (bf16[64,1536]{1,0:T(8,128)(2,1)S(1)}, bf16[64,768]{1,0:T(8,128)(2,1)S(1)}, bf16[768,1536]{1,0:T(8,128)(2,1)S(1)}) custom-call(bf16[64,768]{1,0:T(8,128)(2,1)S(1)} %copy-done.1, bf16[768,1536]{1,0:T(8,128)(2,1)} %w_ref.1, bf16[64,1536]{1,0:T(8,128)(2,1)S(1)} %copy-done), custom_call_target="tpu_custom_call" | custom-call | tf_op jit(solution)/shard_map/updown/pallas_call | solution.py:344
  76.5 1.5 %leave.1 = (bf16[64,1536]{1,0:T(8,128)(2,1)}, bf16[64,768]{1,0:T(8,128)(2,1)}, bf16[768,1536]{1,0:T(8,128)(2,1)}) custom-call(bf16[64,1536]{1,0:T(8,128)(2,1)S(1)} %get-tuple-element.6.refs_0_, bf16[64,768]{1,0:T(8,128)(2,1)S(1)} %get-tuple-element.7.refs_1_, bf16[768,1536]{1,0:T(8,128)(2,1)S(1)} %get-tuple-element.8.refs_2_), custom_call_target="tpu_custom_call" | custom-call | tf_op jit(solution)/shard_map/leave/pallas_call | solution.py:390
Async XLA Ops:
  0.6 0.9 %copy-start = (bf16[64,1536]{1,0:T(8,128)(2,1)S(1)}, bf16[64,1536]{1,0:T(8,128)(2,1)}, u32[]{:S(2)}) copy-start(bf16[64,1536]{1,0:T(8,128)(2,1)} %cot_ref.1) | copy-start | bytes 589828
  1.6 0.9 %copy-start.1 = (bf16[64,768]{1,0:T(8,128)(2,1)S(1)}, bf16[64,768]{1,0:T(8,128)(2,1)}, u32[]{:S(2)}) copy-start(bf16[64,768]{1,0:T(8,128)(2,1)} %tok_ref.1) | copy-start | bytes 294916

commit v3 on v2

--- a/solution.py
+++ b/solution.py
@@ -18,18 +18,23 @@
 ROWS = 16
 TILE = 512
 
-CUTS = {1: ((0, 1, 2, 3, 4),), 2: ((0, 1, 2), (3, 4)), 3: ((0, 1, 2), (3,), (4,)), 4: ((0, 1), (2,), (3,), (4,))}
-PIECES = (1, 1, 1, 1)
+CUTS = {
+    1: ((0, 1, 2, 3, 4),), 2: ((0, 1, 2), (3, 4)), 3: ((0, 1, 2), (3,), (4,)), 4: ((0, 1), (2,), (3,), (4,)),
+    5: ((0, 1, 2, 3), (4,)), 6: ((0, 1), (2, 3, 4)), 7: ((0, 1), (2, 3), (4,)),
+}
+NEED = (4, 3, -3, 2, -2, 1, -1, 0)
+PIECES = (2, 2, 2, 3)
 TWO = (1, 1, 1, 1)
 DIRECT = (0, 0, 0, 0)
 ORDER = (
     ("O", 0), ("O", 1), ("O", 2), ("O", 3), ("F", 0), ("F", 1), ("F", 2), ("F", 3), ("M", 0), ("M", 1),
     ("R4", 0), ("M", 2), ("R4", 1), ("M", 3), ("R3", 0), ("R4", 2), ("R3", 1), ("R4", 3), ("R2", 0), ("R3", 2),
     ("R2", 1), ("R3", 3), ("R1", 0), ("R2", 2), ("R1", 1), ("R2", 3), ("R0", 0), ("R1", 2), ("R0", 1),
-    ("R1", 3), ("A1", 0), ("R0", 2), ("A1", 1), ("R0", 3), ("A2", 0), ("A1", 2), ("A2", 1), ("A1", 3),
-    ("A3", 0), ("A2", 2), ("A3", 1), ("A2", 3), ("A4", 0), ("A3", 2), ("A4", 1), ("A3", 3), ("N0", 0),
-    ("A4", 2), ("N0", 1), ("A4", 3), ("N0", 2), ("WG", 0), ("P", 0), ("N0", 3), ("P", 1), ("P", 2), ("P", 3),
-    ("WG", 1), ("FIN", 0), ("FIN", 1), ("FIN", 2), ("FIN", 3),
+    ("R1", 3), ("A1", 0), ("R0", 2), ("A1", 1), ("R0", 3), ("A2", 0), ("A1", 2), ("A2", 1), ("N0", 0),
+    ("A1", 3), ("N0", 1), ("A3", 0), ("A2", 2), ("A3", 1), ("A2", 3), ("N0", 2), ("A4", 0), ("N0", 3),
+    ("A3", 2), ("A4", 1), ("N1", 0), ("A3", 3), ("N1", 1), ("N1", 3), ("A4", 2), ("WG", 0), ("A4", 3),
+    ("N1", 2), ("P", 0), ("N2", 3), ("P", 1), ("P", 2), ("P", 3), ("WG", 1), ("FIN", 0), ("FIN", 1), ("FIN", 2),
+    ("FIN", 3),
 )
 
 
@@ -68,6 +73,11 @@
         dx, dy = da + k * (db - da), db + k * (da - db)
         return lax.rem(c // 4 + dy + 4, 4) * 4 + lax.rem(c + dx + 4, 4)
 
+    def offsets(dest):
+        dx = lax.rem(lax.rem(dest, 4) - lax.rem(c, 4) + 4, 4)
+        dy = lax.rem(dest // 4 - c // 4 + 4, 4)
+        return dx + k * (dy - dx), dy + k * (dx - dy)
+
     def at_z(q):
         return lax.rem(z + q + NZ, NZ)
 
@@ -129,18 +139,21 @@
         left = tok[s].reshape(NC * ROWS, width)
         part = jnp.dot(left, w[...], preferred_element_type=F32).astype(BF16)
         pp[s] = part.reshape(NZ, 2, ROWS, hidden)
-        remote(pp.at[s, :, other], px.at[s], px_send.at[s], px_recv.at[s], partner)
+        for q in NEED:
+            d = at_z(q)
+            remote(pp.at[s, d, other], px.at[s, d], px_send.at[s], px_recv.at[s, abs(q)], partner)
 
     def base(s, d):
         return pp[s, d, k].astype(F32) + px[s, d].astype(F32)
 
     def r4(s):
-        wait_for(px.at[s], px_recv.at[s])
+        wait_for(px.at[s, 0], px_recv.at[s, 4])
         s4[s] = base(s, at_z(4)).astype(BF16)
         remote(s4.at[s, :, lo], rp.at[s, 3, :, lo], rs_send.at[s, 0], rp_recv.at[s, 3], up)
         remote(s4.at[s, :, hi], rm.at[s, 3, :, hi], rs_send.at[s, 1], rm_recv.at[s, 3], down)
 
     def r3(s):
+        wait_for(px.at[s, pl.ds(0, 2)], px_recv.at[s, 3])
         wait_for(rp.at[s, 3, :, lo], rp_recv.at[s, 3])
         up_sum = base(s, at_z(3))
         sp[s, 3, :, lo] = (up_sum[:, :half] + rp[s, 3, :, lo].astype(F32)).astype(BF16)
@@ -153,6 +166,7 @@
         remote(sm.at[s, 3], rm.at[s, 2], rs_send.at[s, 3], rm_recv.at[s, 2], down)
 
     def rj(s, j):
+        wait_for(px.at[s, pl.ds(0, 2)], px_recv.at[s, j])
         wait_for(rp.at[s, j], rp_recv.at[s, j])
         sp[s, j] = (base(s, at_z(j)) + rp[s, j].astype(F32)).astype(BF16)
         remote(sp.at[s, j], rp.at[s, j - 1], rs_send.at[s, 8 - 2 * j], rp_recv.at[s, j - 1], up)
@@ -161,6 +175,7 @@
         remote(sm.at[s, j], rm.at[s, j - 1], rs_send.at[s, 9 - 2 * j], rm_recv.at[s, j - 1], down)
 
     def r0(s):
+        wait_for(px.at[s, 0], px_recv.at[s, 0])
         wait_for(rp.at[s, 0], rp_recv.at[s, 0])
         wait_for(rm.at[s, 0], rm_recv.at[s, 0])
         if s == 0:
@@ -198,19 +213,6 @@
         wait_for(g.at[s, at_z(4), k, :, hi], gm_recv.at[s, 3])
         remote(far, far, pt_send.at[s], pt_recv.at[s, 7], partner)
 
-    def spread(s):
-        left = g[s].reshape(NR * ROWS, hidden)
-        part = lax.dot_general(
-            left, w[...], (((1,), (1,)), ((), ())), preferred_element_type=F32
-        ).astype(BF16)
-        ip[s] = part.reshape(NC, ROWS, width)
-        for i in (1, 3, 2):
-            for j in range(4):
-                remote(
-                    ip.at[s, shift(i, j)], r2.at[s, 4 * i - 4 + j],
-                    r2_send.at[s], r2_recv.at[s], (r, shift(i, 0)),
-                )
-
     def pass_on(s):
         wait_for(r2.at[s, pl.ds(0, 12)], r2_recv.at[s])
         for j in (1, 3, 2, 0):
@@ -226,25 +228,37 @@
     def m2_part(s, chunks):
         for q, slot in chunks:
             wait_for(g.at[s, 0, 0], pt_recv.at[s, slot])
-        if TWO[s]:
-            return spread(s)
-        left = jnp.concatenate(
-            [g[s, at_z(q)].reshape(2 * ROWS, hidden) for q, _ in chunks], axis=0
-        )
+        if len(chunks) == NZ:
+            left = g[s].reshape(NR * ROWS, hidden)
+        else:
+            left = jnp.concatenate(
+                [g[s, at_z(q)].reshape(2 * ROWS, hidden) for q, _ in chunks], axis=0
+            )
         part = lax.dot_general(
             left, w[...], (((1,), (1,)), ((), ())), preferred_element_type=F32
         ).astype(BF16)
         part = part.reshape(len(chunks), 2, ROWS, width)
+        if len(chunks) == NZ:
+            ip[s] = part.reshape(NC, ROWS, width)
         for n, (q, _) in enumerate(chunks):
             d = at_z(q)
-            ip[s, pl.ds(2 * d, 2)] = part[n]
+            if len(chunks) < NZ:
+                ip[s, pl.ds(2 * d, 2)] = part[n]
             for m in range(2):
                 dest = 2 * d + m
-
-                @pl.when(dest != c)
-                def _():
-                    slot = lax.rem(dest - c + NC, NC) - 1
-                    remote(ip.at[s, dest], r2.at[s, slot], r2_send.at[s], r2_recv.at[s], (r, dest))
+                if TWO[s]:
+                    i, j = offsets(dest)
+
+                    @pl.when(i != 0)
+                    def _():
+                        slot = 4 * i - 4 + j
+                        remote(ip.at[s, dest], r2.at[s, slot], r2_send.at[s], r2_recv.at[s], (r, shift(i, 0)))
+                else:
+
+                    @pl.when(dest != c)
+                    def _():
+                        slot = lax.rem(dest - c + NC, NC) - 1
+                        remote(ip.at[s, dest], r2.at[s, slot], r2_send.at[s], r2_recv.at[s], (r, dest))
 
     def fin(s):
         if TWO[s]:
@@ -371,7 +385,7 @@
             vmem((width, hidden), BF16),
             vmem((width, hidden), F32),
             dma((2 + stages,)), dma((3,)),
-            dma((stages,)), dma((stages, 3)), dma((stages,)), dma((stages,)), dma((stages,)),
+            dma((stages,)), dma((stages, 3)), dma((stages,)), dma((stages,)), dma((stages, 5)),
             dma((stages, 8)), dma((stages, 4)), dma((stages, 4)),
             dma((stages, 8)), dma((stages, 4)), dma((stages, 4)),
             dma((stages,)), dma((stages, 8)),
@@ -385,6 +399,9 @@
 
 
 def on_device(tokens, weight, cotangent):
+    tokens, weight, cotangent = (
+        pltpu.with_memory_space_constraint(v, pltpu.HBM) for v in (tokens, weight, cotangent)
+    )
     outs = kern(tokens, weight, cotangent)
     any_spec, dma = pl.BlockSpec(memory_space=pl.ANY), pltpu.SemaphoreType.DMA
     return tuple(pl.pallas_call(

time: 78.4 us -> 72.9 us (0.930)
  Pallas kernels: 75.5 us -> 72.2 us
  local copies, waits for them, and re-layouts: 1.81 us -> 0 us
    pallas_call x1, Pallas kernels: 74 us -> 70.6 us  [kern(): pl.pallas_call(functools.partial(kernel, stages), out_shape=(jax.ShapeDty...]
    unnamed x4 -> x0, local copies, waits for them, and re-layouts: 1.81 us -> none
where the time goes in v3:
time: 72.9 us; the launch traced here: 72.8 us
  Pallas kernels  72.2 us (99%)
    pallas_call x1, Pallas kernels, kern(): pl.pallas_call(functools.partial(kernel, stages), out_shape=(jax.ShapeDty...  70.6 us
    pallas_call x1, Pallas kernels, on_device(): pl.pallas_call(copy_kernel, out_shape=tuple((jax.ShapeDtypeStruct(o.shape...  1.53 us

profile of v3, /device:TPU:6, one launch (start us, length us, event | category | flops | bytes accessed | tf_op | source)
XLA Modules:
  0.0 72.8 jit_solution(17151429719298382788)
XLA Ops:
  0.6 70.6 %updown.1 = (bf16[64,1536]{1,0:T(8,128)(2,1)S(1)}, bf16[64,768]{1,0:T(8,128)(2,1)S(1)}, bf16[768,1536]{1,0:T(8,128)(2,1)S(1)}) custom-call(bf16[64,768]{1,0:T(8,128)(2,1)} %tok_ref.1, bf16[768,1536]{1,0:T(8,128)(2,1)} %w_ref.1, bf16[64,1536]{1,0:T(8,128)(2,1)} %cot_ref.1), custom_call_target="tpu_custom_call" | custom-call | tf_op jit(solution)/shard_map/updown/pallas_call | solution.py:358
  71.3 1.5 %leave.1 = (bf16[64,1536]{1,0:T(8,128)(2,1)}, bf16[64,768]{1,0:T(8,128)(2,1)}, bf16[768,1536]{1,0:T(8,128)(2,1)}) custom-call(bf16[64,1536]{1,0:T(8,128)(2,1)S(1)} %get-tuple-element.6.refs_0_, bf16[64,768]{1,0:T(8,128)(2,1)S(1)} %get-tuple-element.7.refs_1_, bf16[768,1536]{1,0:T(8,128)(2,1)S(1)} %get-tuple-element.8.refs_2_), custom_call_target="tpu_custom_call" | custom-call | tf_op jit(solution)/shard_map/leave/pallas_call | solution.py:407

commit v4 on v3

--- a/solution.py
+++ b/solution.py
@@ -27,14 +27,14 @@
 TWO = (1, 1, 1, 1)
 DIRECT = (0, 0, 0, 0)
 ORDER = (
-    ("O", 0), ("O", 1), ("O", 2), ("O", 3), ("F", 0), ("F", 1), ("F", 2), ("F", 3), ("M", 0), ("M", 1),
-    ("R4", 0), ("M", 2), ("R4", 1), ("M", 3), ("R3", 0), ("R4", 2), ("R3", 1), ("R4", 3), ("R2", 0), ("R3", 2),
+    ("O", 0), ("O", 1), ("O", 2), ("O", 3), ("F", 0), ("F", 1), ("F", 2), ("F", 3), ("M", 0), ("R4", 0),
+    ("M", 1), ("R4", 1), ("R3", 0), ("M", 2), ("R4", 2), ("R3", 1), ("M", 3), ("R4", 3), ("R2", 0), ("R3", 2),
     ("R2", 1), ("R3", 3), ("R1", 0), ("R2", 2), ("R1", 1), ("R2", 3), ("R0", 0), ("R1", 2), ("R0", 1),
     ("R1", 3), ("A1", 0), ("R0", 2), ("A1", 1), ("R0", 3), ("A2", 0), ("A1", 2), ("A2", 1), ("N0", 0),
     ("A1", 3), ("N0", 1), ("A3", 0), ("A2", 2), ("A3", 1), ("A2", 3), ("N0", 2), ("A4", 0), ("N0", 3),
-    ("A3", 2), ("A4", 1), ("N1", 0), ("A3", 3), ("N1", 1), ("N1", 3), ("A4", 2), ("WG", 0), ("A4", 3),
-    ("N1", 2), ("P", 0), ("N2", 3), ("P", 1), ("P", 2), ("P", 3), ("WG", 1), ("FIN", 0), ("FIN", 1), ("FIN", 2),
-    ("FIN", 3),
+    ("A3", 2), ("A4", 1), ("N1", 0), ("A3", 3), ("N1", 1), ("N1", 3), ("A4", 2), ("A4", 3), ("N1", 2),
+    ("N2", 3), ("P", 0), ("P", 1), ("WG", 0), ("P", 2), ("P", 3), ("WG", 1), ("W", 0), ("FIN", 0), ("FIN", 1),
+    ("FIN", 2), ("FIN", 3),
 )
 
 
@@ -91,6 +91,12 @@
     def wait_for(ref, sem):
         pltpu.make_async_copy(ref, ref, sem).wait()
 
+    own_copies = [
+        pltpu.make_async_copy(tok_ref.at[pl.ds(s * ROWS, ROWS)], tok.at[s, c], in_sem.at[2 + s])
+        for s in range(stages)
+    ]
+    for cp in own_copies:
+        cp.start()
     loads = [
         pltpu.make_async_copy(w_ref, w, in_sem.at[0]),
         pltpu.make_async_copy(cot_ref, cot, in_sem.at[1]),
@@ -108,33 +114,28 @@
         pl.semaphore_signal(barrier, inc=1, device_id=dev, device_id_type=MESH)
     pl.semaphore_wait(barrier, len(greeted))
 
-    own_copies = {}
-
     def own(s):
-        block = tok_ref.at[pl.ds(s * ROWS, ROWS)]
+        own_copies[s].wait()
+        block = tok.at[s, c]
         if DIRECT[s]:
             for i in range(1, NC):
                 remote(block, tok.at[s, c], ag1_send.at[s], ag1b_recv.at[s], (r, peer(i)))
         else:
-            for i in (1, 3, 2):
+            for i in (2, 1, 3):
                 remote(block, tok.at[s, c], ag1_send.at[s], ag1a_recv.at[s, i - 1], (r, shift(i, 0)))
-            for i in (1, 3, 2):
+            for i in (2, 1, 3):
                 remote(block, tok.at[s, c], ag1_send.at[s], ag1b_recv.at[s], (r, shift(0, i)))
-        cp = pltpu.make_async_copy(block, tok.at[s, c], in_sem.at[2 + s])
-        cp.start()
-        own_copies[s] = cp
 
     def forward(s):
-        for i in (1, 3, 2):
+        for i in (2, 1, 3):
             block = tok.at[s, shift(-i, 0)]
             wait_for(block, ag1a_recv.at[s, i - 1])
-            for j in (1, 3, 2):
+            for j in (2, 1, 3):
                 remote(block, block, ag1_send.at[s], ag1b_recv.at[s], (r, shift(0, j)))
 
     def m1(s):
         if s == 0:
             loads[0].wait()
-        own_copies[s].wait()
         wait_for(tok.at[s, pl.ds(0, 15 if DIRECT[s] else 12)], ag1b_recv.at[s])
         left = tok[s].reshape(NC * ROWS, width)
         part = jnp.dot(left, w[...], preferred_element_type=F32).astype(BF16)
@@ -167,11 +168,12 @@
 
     def rj(s, j):
         wait_for(px.at[s, pl.ds(0, 2)], px_recv.at[s, j])
+        up_sum, down_sum = base(s, at_z(j)), base(s, at_z(-j))
         wait_for(rp.at[s, j], rp_recv.at[s, j])
-        sp[s, j] = (base(s, at_z(j)) + rp[s, j].astype(F32)).astype(BF16)
+        sp[s, j] = (up_sum + rp[s, j].astype(F32)).astype(BF16)
         remote(sp.at[s, j], rp.at[s, j - 1], rs_send.at[s, 8 - 2 * j], rp_recv.at[s, j - 1], up)
         wait_for(rm.at[s, j], rm_recv.at[s, j])
-        sm[s, j] = (base(s, at_z(-j)) + rm[s, j].astype(F32)).astype(BF16)
+        sm[s, j] = (down_sum + rm[s, j].astype(F32)).astype(BF16)
         remote(sm.at[s, j], rm.at[s, j - 1], rs_send.at[s, 9 - 2 * j], rm_recv.at[s, j - 1], down)
 
     def r0(s):
@@ -215,7 +217,7 @@
 
     def pass_on(s):
         wait_for(r2.at[s, pl.ds(0, 12)], r2_recv.at[s])
-        for j in (1, 3, 2, 0):
+        for j in (2, 1, 3, 0):
             total = ip[s, shift(0, j)].astype(F32)
             for i in range(3):
                 total += r2[s, 4 * i + j].astype(F32)
@@ -309,7 +311,23 @@
             outs[0].start()
             outs[1].start()
 
-    step = {"O": own, "F": forward, "M": m1, "R4": r4, "R3": r3, "R0": r0, "A4": a4, "P": pass_on, "FIN": fin, "WG": start_wgrad}
+    def settle(_):
+        for s in range(stages):
+            wait_for(tok.at[s, pl.ds(0, NC - 1)], ag1_send.at[s])
+            wait_for(px.at[s], px_send.at[s])
+            wait_for(s4.at[s, :, lo], rs_send.at[s, 0])
+            wait_for(s4.at[s, :, hi], rs_send.at[s, 1])
+            for j in range(2, 8):
+                wait_for(s4.at[s], rs_send.at[s, j])
+            for j in range(6):
+                wait_for(s4.at[s], ag_send.at[s, j])
+            wait_for(s4.at[s, :, lo], ag_send.at[s, 6])
+            wait_for(s4.at[s, :, hi], ag_send.at[s, 7])
+            wait_for(g.at[s, :, 0], pt_send.at[s])
+            if TWO[s]:
+                wait_for(r2.at[s, pl.ds(0, 12)], r2_send.at[s])
+
+    step = {"O": own, "F": forward, "M": m1, "R4": r4, "R3": r3, "R0": r0, "A4": a4, "P": pass_on, "FIN": fin, "WG": start_wgrad, "W": settle}
     for j in (1, 2):
         step[f"R{j}"] = functools.partial(lambda j, s: rj(s, j), j)
     for j in (1, 2, 3):
@@ -321,19 +339,7 @@
     outs[2].start()
 
     for s in range(stages):
-        wait_for(tok.at[s, pl.ds(0, NC - 1)], ag1_send.at[s])
-        wait_for(px.at[s], px_send.at[s])
-        wait_for(s4.at[s, :, lo], rs_send.at[s, 0])
-        wait_for(s4.at[s, :, hi], rs_send.at[s, 1])
-        for j in range(2, 8):
-            wait_for(s4.at[s], rs_send.at[s, j])
-        for j in range(6):
-            wait_for(s4.at[s], ag_send.at[s, j])
-        wait_for(s4.at[s, :, lo], ag_send.at[s, 6])
-        wait_for(s4.at[s, :, hi], ag_send.at[s, 7])
-        wait_for(g.at[s, :, 0], pt_send.at[s])
         if TWO[s]:
-            wait_for(r2.at[s, pl.ds(0, 12)], r2_send.at[s])
             wait_for(r2.at[s, pl.ds(12, 3)], r2b_send.at[s])
         else:
             wait_for(r2.at[s], r2_send.at[s])

time: 72.9 us -> 71.2 us (0.977)
  Pallas kernels: 72.2 us -> 70.4 us
    pallas_call x1, Pallas kernels: 70.6 us -> 68.9 us  [kern(): pl.pallas_call(functools.partial(kernel, stages), out_shape=(jax.ShapeDty...]
where the time goes in v4:
time: 71.2 us; the launch traced here: 71 us
  Pallas kernels  70.4 us (99%)
    pallas_call x1, Pallas kernels, kern(): pl.pallas_call(functools.partial(kernel, stages), out_shape=(jax.ShapeDty...  68.9 us
    pallas_call x1, Pallas kernels, on_device(): pl.pallas_call(copy_kernel, out_shape=tuple((jax.ShapeDtypeStruct(o.shape...  1.53 us

profile of v4, /device:TPU:6, one launch (start us, length us, event | category | flops | bytes accessed | tf_op | source)
XLA Modules:
  0.0 71.0 jit_solution(8514703537596884971)
XLA Ops:
  0.6 68.9 %updown.1 = (bf16[64,1536]{1,0:T(8,128)(2,1)S(1)}, bf16[64,768]{1,0:T(8,128)(2,1)S(1)}, bf16[768,1536]{1,0:T(8,128)(2,1)S(1)}) custom-call(bf16[64,768]{1,0:T(8,128)(2,1)} %tok_ref.1, bf16[768,1536]{1,0:T(8,128)(2,1)} %w_ref.1, bf16[64,1536]{1,0:T(8,128)(2,1)} %cot_ref.1), custom_call_target="tpu_custom_call" | custom-call | tf_op jit(solution)/shard_map/updown/pallas_call | solution.py:364
  69.5 1.5 %leave.1 = (bf16[64,1536]{1,0:T(8,128)(2,1)}, bf16[64,768]{1,0:T(8,128)(2,1)}, bf16[768,1536]{1,0:T(8,128)(2,1)}) custom-call(bf16[64,1536]{1,0:T(8,128)(2,1)S(1)} %get-tuple-element.6.refs_0_, bf16[64,768]{1,0:T(8,128)(2,1)S(1)} %get-tuple-element.7.refs_1_, bf16[768,1536]{1,0:T(8,128)(2,1)S(1)} %get-tuple-element.8.refs_2_), custom_call_target="tpu_custom_call" | custom-call | tf_op jit(solution)/shard_map/leave/pallas_call | solution.py:413

commit v5 on v4

--- a/solution.py
+++ b/solution.py
@@ -262,6 +262,10 @@
                         slot = lax.rem(dest - c + NC, NC) - 1
                         remote(ip.at[s, dest], r2.at[s, slot], r2_send.at[s], r2_recv.at[s], (r, dest))
 
+    def leave_sum(s):
+        rows = pl.ds(s * ROWS, ROWS)
+        pltpu.make_async_copy(ig.at[rows], ig_ref.at[rows], out_sem.at[2]).start()
+
     def fin(s):
         if TWO[s]:
             wait_for(r2.at[s, pl.ds(12, 3)], r2b_recv.at[s])
@@ -269,12 +273,13 @@
             for j in range(3):
                 total += r2[s, 12 + j].astype(F32)
             ig[pl.ds(s * ROWS, ROWS)] = total.astype(BF16)
-            return
+            return leave_sum(s)
         wait_for(r2.at[s], r2_recv.at[s])
         total = ip[s, c].astype(F32)
         for i in range(NC - 1):
             total += r2[s, i].astype(F32)
         ig[pl.ds(s * ROWS, ROWS)] = total.astype(BF16)
+        leave_sum(s)
 
     def wgrad(part):
         some = pl.ds(2 * part, 2)
@@ -290,6 +295,7 @@
                 acc[:, cols] = total
             else:
                 wg[:, cols] = (acc[:, cols] + total).astype(BF16)
+                pltpu.make_async_copy(wg.at[:, cols], wg_ref.at[:, cols], out_sem.at[1]).start()
             return carry
 
         lax.fori_loop(0, hidden // TILE, body, 0)
@@ -306,10 +312,9 @@
     ]
 
     def start_wgrad(part):
+        if part == 0:
+            outs[0].start()
         wgrad(part)
-        if part == 1:
-            outs[0].start()
-            outs[1].start()
 
     def settle(_):
         for s in range(stages):
@@ -336,7 +341,6 @@
         step[f"N{n}"] = functools.partial(lambda n, s: product(s, n), n)
     for name, s in ORDER:
         step[name](s)
-    outs[2].start()
 
     for s in range(stages):
         if TWO[s]:

time: 71.2 us -> 71 us (level)
  no operation moved by 1% of the time
where the time goes in v5:
time: 71 us; the launch traced here: 70.9 us
  Pallas kernels  70.3 us (99%)
    pallas_call x1, Pallas kernels, kern(): pl.pallas_call(functools.partial(kernel, stages), out_shape=(jax.ShapeDty...  68.8 us
    pallas_call x1, Pallas kernels, on_device(): pl.pallas_call(copy_kernel, out_shape=tuple((jax.ShapeDtypeStruct(o.shape...  1.53 us

profile of v5, /device:TPU:6, one launch (start us, length us, event | category | flops | bytes accessed | tf_op | source)
XLA Modules:
  0.0 70.9 jit_solution(10244752456342591567)
XLA Ops:
  0.6 68.8 %updown.1 = (bf16[64,1536]{1,0:T(8,128)(2,1)S(1)}, bf16[64,768]{1,0:T(8,128)(2,1)S(1)}, bf16[768,1536]{1,0:T(8,128)(2,1)S(1)}) custom-call(bf16[64,768]{1,0:T(8,128)(2,1)} %tok_ref.1, bf16[768,1536]{1,0:T(8,128)(2,1)} %w_ref.1, bf16[64,1536]{1,0:T(8,128)(2,1)} %cot_ref.1), custom_call_target="tpu_custom_call" | custom-call | tf_op jit(solution)/shard_map/updown/pallas_call | solution.py:368
  69.4 1.5 %leave.1 = (bf16[64,1536]{1,0:T(8,128)(2,1)}, bf16[64,768]{1,0:T(8,128)(2,1)}, bf16[768,1536]{1,0:T(8,128)(2,1)}) custom-call(bf16[64,1536]{1,0:T(8,128)(2,1)S(1)} %get-tuple-element.6.refs_0_, bf16[64,768]{1,0:T(8,128)(2,1)S(1)} %get-tuple-element.7.refs_1_, bf16[768,1536]{1,0:T(8,128)(2,1)S(1)} %get-tuple-element.8.refs_2_), custom_call_target="tpu_custom_call" | custom-call | tf_op jit(solution)/shard_map/leave/pallas_call | solution.py:417
